TPU v7x, 32 devices: a whole 2x2x4 slice. The times are simulated.
32 devices in a mesh: gx: 2 (over x), gy: 4 (over z), gz: 4 (over y, core).
Axes of the slice: x: 2, y: 2, z: 4, core: 2. Of those that a mesh axis runs over, the one named last changes fastest.
Arguments:
- pressure: float32 [2, 32, 32, 512], P(None, 'gx', 'gy', 'gz'), may hold values from -6 to 6
- saturation: float32 [3, 2, 32, 32, 512], P(None, None, 'gx', 'gy', 'gz'), may hold values from 0.15 to 0.45
- permeability: float32 [32, 32, 512], P('gx', 'gy', 'gz'), may hold values from 0.5 to 2
- porosity: float32 [32, 32, 512], P('gx', 'gy', 'gz'), may hold values from 0.1 to 0.35
- upwind_flags: int32 [32, 32, 512], P('gx', 'gy', 'gz'), may hold values from 0 to 63
- diag_inverse: float32 [2, 3, 3, 32, 32, 512], P(None, None, None, 'gx', 'gy', 'gz'), may hold values from -0.12 to 0.8, as said below
- seismic_obs: float32 [32, 32, 512], P('gx', 'gy', 'gz'), may hold values from -6 to 6
- well_x: int32 [2, 4, 64], P('gx', 'gy'), may hold values from 0 to 15
- well_y: int32 [2, 4, 64], P('gx', 'gy'), may hold values from 0 to 7
- well_top: int32 [2, 4, 64], P('gx', 'gy'), may hold values from 0 to 255
- well_len: int32 [2, 4, 64], P('gx', 'gy'), may hold values from 128 to 256
- well_bhp: float32 [2, 2, 4, 64], P(None, 'gx', 'gy'), may hold values from -3 to 3
- well_obs: float32 [2, 2, 4, 64], P(None, 'gx', 'gy'), may hold values from -48 to 48
- fault_cell: int32 [32, 16, 128], P(('gx', 'gy', 'gz')), may hold values from 0 to 16383
- fault_count: int32 [32, 16], P(('gx', 'gy', 'gz')), may hold values from 0 to 128, as said below
- fault_trans: float32 [32, 16, 128], P(('gx', 'gy', 'gz')), may hold values from 0.5 to 2, as said below
- fault_up: int32 [32, 16, 128], P(('gx', 'gy', 'gz')), may hold values from 0 to 3, as said below
- region_map: int32 [8, 8, 128], P('gx', 'gy', 'gz'), may hold values from 0 to 1023
Outputs:
- adjoint: float32 [2, 3, 32, 32, 512], P(None, None, 'gx', 'gy', 'gz')
- region_grad: float32 [2, 1024], P(None, ('gx', 'gy', 'gz'))
Inputs may be any that keep to these rules, and one draw needn't show every extreme that they name: fault_count[dev][p] equals fault_count[i * 16 + p][a] of the connection's other end; a device has no connections with itself; in every draw one device of each group of 16 has exactly 128 connections with every other device of its group. `fault_cell`: slot s of dev toward peer p and slot s of that peer toward dev are the two ends of one connection. `fault_trans`: both ends of a connection hold the same transmissibility. `fault_up`: the two ends of a connection hold opposite bits. `diag_inverse`: entries [t][0][0] lie in 0.25 to 0.5, entries [t][u][u] for u = 1, 2 in 0.4 to 0.8, all others in -0.12 to 0.12.
All inputs are finite; a program needn't handle non-finite values.
Results may differ from a plain program's by a relative error of at most 0.0001.
Values sent between devices are 32-bit elements; how exact they have to be, the bound alone decides.
A program may use at most 128 MiB of HBM per device.

v0:
```python
import jax
import jax.numpy as jnp
from jax import lax
from jax.sharding import PartitionSpec as P

ITERS = 6
BOX = 4
PARAM_REGIONS = 32


fluid_viscosity = (0.4, 0.5, 1.0)
sigma_sq = 64.0


def extended_2(block, sides, width):
    for axis, dim in sides:
        count = lax.axis_size(axis)
        forward = [(i, i + 1) for i in range(count - 1)]
        backward = [(target, source) for source, target in forward]
        low = lax.ppermute(
            lax.slice_in_dim(block, block.shape[dim] - width, None, axis=dim), axis, forward
        )
        high = lax.ppermute(lax.slice_in_dim(block, 0, width, axis=dim), axis, backward)
        block = jnp.concatenate([low, block, high], axis=dim)
    return block


def phase_mobility(water_sat, oil_sat):
    gas_sat = 1.0 - water_sat - oil_sat
    return jnp.stack(
        [
            water_sat * water_sat / fluid_viscosity[0],
            oil_sat * oil_sat / fluid_viscosity[1],
            gas_sat * gas_sat / fluid_viscosity[2],
        ]
    )


def mobility_slopes(water_sat, oil_sat):
    gas_sat = 1.0 - water_sat - oil_sat
    return (
        2.0 * water_sat / fluid_viscosity[0] - 2.0 * gas_sat / fluid_viscosity[2],
        2.0 * oil_sat / fluid_viscosity[1] - 2.0 * gas_sat / fluid_viscosity[2],
    )


def interior_strip(padded, direction):
    slicer = [slice(None), slice(1, -1), slice(1, -1), slice(1, -1)]
    slicer[direction + 1] = slice(None)
    return padded[tuple(slicer)]


def apply_inverse(inverse, residual):
    return jnp.sum(inverse * residual[:, None], axis=0)


def box_sums(quantity):
    shaped = quantity.reshape(
        quantity.shape[0] // BOX, BOX, quantity.shape[1] // BOX, BOX, quantity.shape[2] // BOX, BOX
    )
    return jnp.sum(shaped, axis=(1, 3, 5)).reshape(-1)


def fault_exchange(values):
    return lax.all_to_all(values, ("gy", "gz"), split_axis=1, concat_axis=1, tiled=True)


def fault_sum(lagrange, coefficient, cell_index):
    flattened = lagrange.reshape(lagrange.shape[0], -1)
    own_values = flattened[:, cell_index]
    arrived = fault_exchange(own_values)
    contribution = jnp.sum(coefficient * arrived, axis=0)
    faults = (
        jnp.zeros((flattened.shape[1],), jnp.float32)
        .at[cell_index.reshape(-1)]
        .add(contribution.reshape(-1))
    )
    return faults.reshape(lagrange.shape[1:])


def neighbour_terms(lagrange, ahead_list, behind_list, want_local):
    padded = extended_2(lagrange, (("gx", 1), ("gy", 2), ("gz", 3)), 1)
    upper_terms = []
    lower_terms = []
    for direction in range(3):
        stripe = interior_strip(padded, direction)
        length = lagrange.shape[direction + 1]
        upper_terms.append(
            jnp.sum(
                ahead_list[direction] * lax.slice_in_dim(stripe, 2, length + 2, axis=direction + 1),
                axis=0,
            )
        )
        lower_terms.append(
            jnp.sum(
                behind_list[direction] * lax.slice_in_dim(stripe, 0, length, axis=direction + 1),
                axis=0,
            )
        )
    local_ahead = None
    local_behind = None
    if want_local:
        local_ahead = [jnp.sum(coefficient * lagrange, axis=0) for coefficient in ahead_list]
        local_behind = [jnp.sum(coefficient * lagrange, axis=0) for coefficient in behind_list]
    return (upper_terms, lower_terms, local_ahead, local_behind)


def local(
    pressure,
    saturation,
    permeability,
    porosity,
    upwind_flags,
    diag_inverse,
    seismic_obs,
    well_x,
    well_y,
    well_top,
    well_len,
    well_bhp,
    well_obs,
    fault_cell,
    fault_count,
    fault_trans,
    fault_up,
    region_map,
):
    mobility = [
        phase_mobility(saturation[step_index + 1, 0], saturation[step_index + 1, 1])
        for step_index in range(2)
    ]
    flag_field = upwind_flags.astype(jnp.float32)[None]
    bundle = jnp.concatenate(
        [permeability[None], mobility[0], mobility[1], flag_field, pressure], axis=0
    )
    padded = extended_2(bundle, (("gx", 1), ("gy", 2), ("gz", 3)), 1)
    ahead_coef = [[], []]
    behind_coef = [[], []]
    pressure_ahead = [[], []]
    pressure_trailing = [[], []]
    for direction in range(3):
        stripe = interior_strip(padded, direction)
        length = permeability.shape[direction]
        lower_side = lax.slice_in_dim(stripe, 0, length + 1, axis=direction + 1)
        upper_side = lax.slice_in_dim(stripe, 1, length + 2, axis=direction + 1)
        face_trans = jnp.sqrt(lower_side[0] * upper_side[0])
        lower_flags = lower_side[7].astype(jnp.int32)
        for step_index in range(2):
            first = 1 + 3 * step_index
            upwind_bit = jnp.bitwise_and(
                jnp.right_shift(lower_flags, 3 * step_index + direction), 1
            )
            chosen = jnp.where(
                upwind_bit[None] == 1, lower_side[first : first + 3], upper_side[first : first + 3]
            )
            extended = face_trans[None] * chosen
            ahead_coef[step_index].append(
                lax.slice_in_dim(extended, 1, length + 1, axis=direction + 1)
            )
            behind_coef[step_index].append(
                lax.slice_in_dim(extended, 0, length, axis=direction + 1)
            )
            pressure_stripe = stripe[8 + step_index]
            pressure_ahead[step_index].append(
                lax.slice_in_dim(pressure_stripe, 2, length + 2, axis=direction)
            )
            pressure_trailing[step_index].append(
                lax.slice_in_dim(pressure_stripe, 0, length, axis=direction)
            )
    cell_index = fault_cell[0]
    live_slots = (
        jnp.arange(cell_index.shape[1], dtype=jnp.int32)[None, :] < fault_count[0][:, None]
    ).astype(jnp.float32)
    own_mobility = jnp.concatenate(mobility, axis=0).reshape(6, -1)[:, cell_index]
    peer_mobility = lax.all_to_all(
        own_mobility, ("gy", "gz"), split_axis=1, concat_axis=1, tiled=True
    )
    fault_coef = []
    for step_index in range(2):
        upwind_bit = jnp.bitwise_and(jnp.right_shift(fault_up[0], step_index), 1)
        first = 3 * step_index
        chosen = jnp.where(
            upwind_bit[None] == 1, own_mobility[first : first + 3], peer_mobility[first : first + 3]
        )
        fault_coef.append(fault_trans[0][None] * chosen * live_slots[None])
    column_x = well_x[0, 0]
    column_y = well_y[0, 0]
    depth_count = permeability.shape[2]
    depth_index = (lax.axis_index("gz") * depth_count + jnp.arange(depth_count, dtype=jnp.int32))[
        None, :
    ]
    top_cells = well_top[0, 0][:, None]
    perforated = (
        (depth_index >= top_cells) & (depth_index < top_cells + well_len[0, 0][:, None])
    ).astype(jnp.float32)
    column_perm = permeability[column_x, column_y]
    partial_rates = []
    column_data = []
    for step_index in range(2):
        column_pressure = pressure[step_index][column_x, column_y]
        column_total = jnp.sum(mobility[step_index][:, column_x, column_y], axis=0)
        drawdown = column_pressure - well_bhp[step_index, 0, 0][:, None]
        partial_rates.append(jnp.sum(perforated * column_perm * column_total * drawdown, axis=1))
        column_data.append((column_total, drawdown))
    well_flow_rates = lax.psum(jnp.stack(partial_rates), "gz")
    misfit = (well_flow_rates - well_obs[:, 0, 0]) / sigma_sq
    sources = []
    explicit = jnp.zeros(permeability.shape, jnp.float32)
    for step_index in range(2):
        column_total, drawdown = column_data[step_index]
        water_slope, oil_slope = mobility_slopes(
            saturation[step_index + 1, 0][column_x, column_y],
            saturation[step_index + 1, 1][column_x, column_y],
        )
        weight = misfit[step_index][:, None] * column_perm * perforated
        added = jnp.stack(
            [weight * column_total, weight * drawdown * water_slope, weight * drawdown * oil_slope]
        )
        sources.append(
            jnp.zeros((3,) + permeability.shape, jnp.float32).at[:, column_x, column_y].add(added)
        )
        explicit = explicit.at[column_x, column_y].add(weight * column_total * drawdown)
    sources[1] = sources[1].at[1].add(saturation[2, 0] - seismic_obs)

    def solve(step_index, source):
        lagrange = apply_inverse(diag_inverse[step_index], source)
        for sweep_index in range(ITERS - 1):
            upper_terms, lower_terms, spare_leading, unused_behind = neighbour_terms(
                lagrange, ahead_coef[step_index], behind_coef[step_index], False
            )
            face_total = (
                upper_terms[0]
                + lower_terms[0]
                + upper_terms[1]
                + lower_terms[1]
                + upper_terms[2]
                + lower_terms[2]
            )
            coupling = face_total + fault_sum(lagrange, fault_coef[step_index], cell_index)
            residual = jnp.concatenate([(source[0] + coupling)[None], source[1:]], axis=0)
            lagrange = apply_inverse(diag_inverse[step_index], residual)
        return lagrange

    late = solve(1, sources[1])
    early_source = sources[0] + jnp.stack(
        [jnp.zeros_like(porosity), porosity * (late[0] - late[2]), porosity * (late[1] - late[2])]
    )
    early = solve(0, early_source)
    solved = [early, late]
    flux_list = []
    porosity_terms = []
    for step_index in (1, 0):
        lagrange = solved[step_index]
        upper_terms, lower_terms, local_ahead, local_behind = neighbour_terms(
            lagrange, ahead_coef[step_index], behind_coef[step_index], True
        )
        pressure_here = pressure[step_index]
        flux_grad = jnp.zeros_like(pressure_here)
        for direction in range(3):
            flux_grad = (
                flux_grad
                + 0.5
                * (pressure_here - pressure_ahead[step_index][direction])
                * (local_ahead[direction] - upper_terms[direction])
                + 0.5
                * (pressure_trailing[step_index][direction] - pressure_here)
                * (lower_terms[direction] - local_behind[direction])
            )
        flux_list.append(flux_grad)
        water_change = saturation[step_index + 1, 0] - saturation[step_index, 0]
        oil_change = saturation[step_index + 1, 1] - saturation[step_index, 1]
        porosity_terms.append(
            lagrange[0] * water_change
            + lagrange[1] * oil_change
            - lagrange[2] * (water_change + oil_change)
        )
    log_perm_grad = explicit - (flux_list[0] + flux_list[1])
    porosity_gradient = -(porosity_terms[0] + porosity_terms[1])
    box_totals = jnp.stack([box_sums(log_perm_grad), box_sums(porosity_gradient)], axis=1)
    region_labels = PARAM_REGIONS * lax.axis_size("gx") * lax.axis_size("gy") * lax.axis_size("gz")
    region_partial = jax.ops.segment_sum(
        box_totals, region_map.reshape(-1), num_segments=region_labels
    ).T
    region_grad = lax.psum_scatter(
        region_partial, ("gx", "gy", "gz"), scatter_dimension=1, tiled=True
    )
    return (jnp.stack([early, late]), region_grad)


def solution(mesh):
    placed = (
        P(None, "gx", "gy", "gz"),
        P(None, None, "gx", "gy", "gz"),
        P("gx", "gy", "gz"),
        P("gx", "gy", "gz"),
        P("gx", "gy", "gz"),
        P(None, None, None, "gx", "gy", "gz"),
        P("gx", "gy", "gz"),
        P("gx", "gy", None),
        P("gx", "gy", None),
        P("gx", "gy", None),
        P("gx", "gy", None),
        P(None, "gx", "gy", None),
        P(None, "gx", "gy", None),
        P(("gx", "gy", "gz"), None, None),
        P(("gx", "gy", "gz"), None),
        P(("gx", "gy", "gz"), None, None),
        P(("gx", "gy", "gz"), None, None),
        P("gx", "gy", "gz"),
    )
    return jax.shard_map(
        local,
        mesh=mesh,
        in_specs=placed,
        out_specs=(P(None, None, "gx", "gy", "gz"), P(None, ("gx", "gy", "gz"))),
        check_vma=False,
    )
```

profile of v0, /device:TPU:0, one launch (start us, length us, event | category | flops | bytes accessed | tf_op | source)
XLA Modules:
  0.0 1038.9 jit_solution(6294457973169037684)
XLA Ops:
  40.4 11.0 %gather_fusion.8 = f32[2048,3]{1,0:T(8,128)} fusion(f32[3,16384]{0,1:T(8,128)} %bitcast.380, s32[2048]{0:T(1024)S(1)} %fusion.262), kind=kCustom, calls=%fused_computation.8 | custom fusion | bytes 57344 | tf_op jit(solution)/shard_map/gather | solution.py:70
  83.9 11.0 %gather_fusion.7 = f32[2048,6]{1,0:T(8,128)} fusion(f32[6,16384]{0,1:T(8,128)} %copy.142, s32[2048]{0:T(1024)S(1)} %fusion.262), kind=kCustom, calls=%fused_computation.7 | custom fusion | bytes 106496 | tf_op jit(solution)/shard_map/gather | solution.py:174
  123.1 12.0 %scatter_custom_fusion.1 = f32[16384]{0:T(1024)} fusion(s32[2048]{0:T(1024)} %bitcast.453, f32[2048]{0:T(1024)S(1)} %bitcast.444, f32[]{:T(128)} %constant.81.clone.1), kind=kCustom, calls=%fused_computation.698 | custom fusion | flops 2048 | bytes 66048 | tf_op jit(solution)/shard_map/scatter-add | solution.py:76
  180.0 11.0 %gather_fusion.9 = f32[2048,3]{1,0:T(8,128)} fusion(f32[3,16384]{0,1:T(8,128)} %bitcast.383, s32[2048]{0:T(1024)S(1)} %fusion.262), kind=kCustom, calls=%fused_computation.9 | custom fusion | bytes 57344 | tf_op jit(solution)/shard_map/gather | solution.py:70
  207.1 12.0 %scatter_custom_fusion.2 = f32[16384]{0:T(1024)} fusion(s32[2048]{0:T(1024)} %bitcast.454, f32[2048]{0:T(1024)S(1)} %bitcast.447, f32[]{:T(128)} %constant.81.clone.1), kind=kCustom, calls=%fused_computation.696 | custom fusion | flops 2048 | bytes 66048 | tf_op jit(solution)/shard_map/scatter-add | solution.py:76
  241.3 11.0 %gather_fusion.10 = f32[2048,3]{1,0:T(8,128)} fusion(f32[3,16384]{0,1:T(8,128)} %bitcast.384, s32[2048]{0:T(1024)S(1)} %fusion.262), kind=kCustom, calls=%fused_computation.10 | custom fusion | bytes 57344 | tf_op jit(solution)/shard_map/gather | solution.py:70
  254.4 11.1 %all-to-all-start.3 = ((f32[3,16,128]{2,0,1:T(4,128)}), f32[3,16,128]{2,0,1:T(4,128)}, u32[]{:S(2)}, u32[]{:S(2)}) async-start(f32[3,16,128]{2,0,1:T(4,128)} %bitcast.436), calls=%async_computation.3 | async-start | bytes 65536 | tf_op jit(solution)/shard_map/all_to_all | solution.py:65
  275.3 12.0 %scatter_custom_fusion.3 = f32[16384]{0:T(1024)} fusion(s32[2048]{0:T(1024)} %bitcast.455, f32[2048]{0:T(1024)S(1)} %bitcast.448, f32[]{:T(128)} %constant.81.clone.1), kind=kCustom, calls=%fused_computation.694 | custom fusion | flops 2048 | bytes 66048 | tf_op jit(solution)/shard_map/scatter-add | solution.py:76
  322.8 11.2 %all-to-all-start.4 = ((f32[3,16,128]{2,0,1:T(4,128)}), f32[3,16,128]{2,0,1:T(4,128)}, u32[]{:S(2)}, u32[]{:S(2)}) async-start(f32[3,16,128]{2,0,1:T(4,128)} %bitcast.437), calls=%async_computation.4 | async-start | bytes 65536 | tf_op jit(solution)/shard_map/all_to_all | solution.py:65
  343.9 12.0 %scatter_custom_fusion.4 = f32[16384]{0:T(1024)} fusion(s32[2048]{0:T(1024)} %bitcast.456, f32[2048]{0:T(1024)S(1)} %bitcast.449, f32[]{:T(128)} %constant.81.clone.1), kind=kCustom, calls=%fused_computation.692 | custom fusion | flops 2048 | bytes 66048 | tf_op jit(solution)/shard_map/scatter-add | solution.py:76
  414.4 11.0 %gather_fusion.12 = f32[2048,3]{1,0:T(8,128)} fusion(f32[3,16384]{0,1:T(8,128)} %bitcast.386, s32[2048]{0:T(1024)S(1)} %fusion.262), kind=kCustom, calls=%fused_computation.12 | custom fusion | bytes 57344 | tf_op jit(solution)/shard_map/gather | solution.py:70
  427.6 11.4 %all-to-all-start.5 = ((f32[3,16,128]{2,0,1:T(4,128)}), f32[3,16,128]{2,0,1:T(4,128)}, u32[]{:S(2)}, u32[]{:S(2)}) async-start(f32[3,16,128]{2,0,1:T(4,128)} %bitcast.438), calls=%async_computation.5 | async-start | bytes 65536 | tf_op jit(solution)/shard_map/all_to_all | solution.py:65
  448.8 12.0 %scatter_custom_fusion.5 = f32[16384]{0:T(1024)} fusion(s32[2048]{0:T(1024)} %bitcast.457, f32[2048]{0:T(1024)S(1)} %bitcast.446, f32[]{:T(128)} %constant.81.clone.1), kind=kCustom, calls=%fused_computation.690 | custom fusion | flops 2048 | bytes 66048 | tf_op jit(solution)/shard_map/scatter-add | solution.py:76
  496.5 11.0 %gather_fusion.15 = f32[2048,3]{1,0:T(8,128)} fusion(f32[3,16384]{0,1:T(8,128)} %bitcast.381, s32[2048]{0:T(1024)S(1)} %fusion.262), kind=kCustom, calls=%fused_computation.15 | custom fusion | bytes 57344 | tf_op jit(solution)/shard_map/gather | solution.py:70
  509.6 11.2 %all-to-all-start.6 = ((f32[3,16,128]{2,0,1:T(4,128)}), f32[3,16,128]{2,0,1:T(4,128)}, u32[]{:S(2)}, u32[]{:S(2)}) async-start(f32[3,16,128]{2,0,1:T(4,128)} %bitcast.434), calls=%async_computation.6 | async-start | bytes 65536 | tf_op jit(solution)/shard_map/all_to_all | solution.py:65
  531.4 12.0 %scatter_custom_fusion.7 = f32[16384]{0:T(1024)} fusion(s32[2048]{0:T(1024)} %bitcast.458, f32[2048]{0:T(1024)S(1)} %bitcast.443, f32[]{:T(128)} %constant.81.clone.1), kind=kCustom, calls=%fused_computation.688 | custom fusion | flops 2048 | bytes 66048 | tf_op jit(solution)/shard_map/scatter-add | solution.py:76
  565.4 11.0 %gather_fusion.16 = f32[2048,3]{1,0:T(8,128)} fusion(f32[3,16384]{0,1:T(8,128)} %bitcast.387, s32[2048]{0:T(1024)S(1)} %fusion.262), kind=kCustom, calls=%fused_computation.16 | custom fusion | bytes 57344 | tf_op jit(solution)/shard_map/gather | solution.py:70
  578.5 11.4 %all-to-all-start.7 = ((f32[3,16,128]{2,0,1:T(4,128)}), f32[3,16,128]{2,0,1:T(4,128)}, u32[]{:S(2)}, u32[]{:S(2)}) async-start(f32[3,16,128]{2,0,1:T(4,128)} %bitcast.113), calls=%async_computation.7 | async-start | bytes 65536 | tf_op jit(solution)/shard_map/all_to_all | solution.py:65
  598.1 11.4 %scatter_custom_fusion.8 = f32[16384]{0:T(1024)S(1)} fusion(s32[2048]{0:T(1024)} %bitcast.459, f32[2048]{0:T(1024)S(1)} %bitcast.450, f32[]{:T(128)} %constant.81.clone.1), kind=kCustom, calls=%fused_computation.686 | custom fusion | flops 2048 | bytes 66048 | tf_op jit(solution)/shard_map/scatter-add | solution.py:76
  685.6 11.4 %scatter_custom_fusion.9 = f32[16384]{0:T(1024)S(1)} fusion(s32[2048]{0:T(1024)} %bitcast.460, f32[2048]{0:T(1024)S(1)} %bitcast.451, f32[]{:T(128)} %constant.81.clone.1), kind=kCustom, calls=%fused_computation.684 | custom fusion | flops 2048 | bytes 66048 | tf_op jit(solution)/shard_map/scatter-add | solution.py:76
  755.3 12.0 %scatter_custom_fusion.10 = f32[16384]{0:T(1024)} fusion(s32[2048]{0:T(1024)} %bitcast.461, f32[2048]{0:T(1024)S(1)} %bitcast.452, f32[]{:T(128)} %constant.81.clone.1), kind=kCustom, calls=%fused_computation.682 | custom fusion | flops 2048 | bytes 66048 | tf_op jit(solution)/shard_map/scatter-add | solution.py:76
  805.5 11.2 %all-to-all-start.10 = ((f32[3,16,128]{2,0,1:T(4,128)}), f32[3,16,128]{2,0,1:T(4,128)S(1)}, u32[]{:S(2)}, u32[]{:S(2)}) async-start(f32[3,16,128]{2,0,1:T(4,128)} %bitcast.131), calls=%async_computation.10 | async-start | bytes 65536 | tf_op jit(solution)/shard_map/all_to_all | solution.py:65
  825.0 11.4 %scatter_custom_fusion.11 = f32[16384]{0:T(1024)S(1)} fusion(s32[2048]{0:T(1024)} %bitcast.462, f32[2048]{0:T(1024)S(1)} %bitcast.445, f32[]{:T(128)} %constant.81.clone.1), kind=kCustom, calls=%fused_computation.680 | custom fusion | flops 2048 | bytes 66048 | tf_op jit(solution)/shard_map/scatter-add | solution.py:76
  889.3 141.0 %reduce-scatter.2.cloned.1.call-done = f32[2,32]{0,1:T(8,128)} async-done(((f32[2,1024]{0,1:T(8,128)}), f32[2,32]{0,1:T(8,128)}) %reduce-scatter.2.cloned.1.call-update) | async-done | bytes 272 | tf_op jit(solution)/shard_map/reduce_scatter | solution.py:284
  (729 shorter events, 617.8 us)
Async XLA Ops:
  53.6 55.2 %all-to-all-start.1 = ((f32[3,16,128]{2,0,1:T(4,128)}), f32[3,16,128]{2,0,1:T(4,128)S(1)}, u32[]{:S(2)}, u32[]{:S(2)}) async-start(f32[3,16,128]{2,0,1:T(4,128)} %bitcast.61), calls=%async_computation.1 | async-start | bytes 65536 | tf_op jit(solution)/shard_map/all_to_all | solution.py:65
  58.7 44.7 %collective-permute-start = (f32[10,1,8,128]{3,2,1,0:T(8,128)S(1)}, f32[10,1,8,128]{3,2,1,0:T(8,128)S(1)}, u32[]{:S(2)}, u32[]{:S(2)}) collective-permute-start(f32[10,1,8,128]{3,2,1,0:T(8,128)S(1)} %get-tuple-element.154), channel_id=1, source_target_pairs={{0,16},{1,17},{2,18},{3,19},{4,20},{5,21},{6,22},{7,23},{8,24},{9,... | collective-permute-start | bytes 122888 | tf_op jit(solution)/shard_map/ppermute | solution.py:20
  62.0 41.3 %collective-permute-start.1 = (f32[10,1,8,128]{3,2,1,0:T(8,128)S(1)}, f32[10,1,8,128]{3,2,1,0:T(8,128)S(1)}, u32[]{:S(2)}, u32[]{:S(2)}) collective-permute-start(f32[10,1,8,128]{3,2,1,0:T(8,128)S(1)} %get-tuple-element.155), channel_id=1, source_target_pairs={{16,0},{17,1},{18,2},{19,3},{20,4},{21,5},{22,6},{23,7},{24,8},{25... | collective-permute-start | bytes 122888 | tf_op jit(solution)/shard_map/ppermute | solution.py:23
  98.1 58.7 %collective-permute-start.10 = (f32[3,18,10,1]{3,2,1,0:T(8,128)}, f32[3,18,10,1]{3,2,1,0:T(8,128)}, u32[]{:S(2)}, u32[]{:S(2)}) collective-permute-start(f32[3,18,10,1]{3,2,1,0:T(8,128)} %get-tuple-element.179), channel_id=1, source_target_pairs={{1,0},{2,1},{3,2},{5,4},{6,5},{7,6},{9,8},{10,9},{11,10},{13,12},{... | collective-permute-start | bytes 6488 | tf_op jit(solution)/shard_map/ppermute | solution.py:23
  99.6 57.3 %collective-permute-start.11 = (f32[3,18,10,1]{3,2,1,0:T(8,128)}, f32[3,18,10,1]{3,2,1,0:T(8,128)}, u32[]{:S(2)}, u32[]{:S(2)}) collective-permute-start(f32[3,18,10,1]{3,2,1,0:T(8,128)} %get-tuple-element.178), channel_id=1, source_target_pairs={{0,1},{1,2},{2,3},{4,5},{5,6},{6,7},{8,9},{9,10},{10,11},{12,13},{... | collective-permute-start | bytes 6488 | tf_op jit(solution)/shard_map/ppermute | solution.py:20
  229.2 36.4 %collective-permute-start.20 = (f32[3,18,1,128]{3,2,1,0:T(1,128)}, f32[3,18,1,128]{3,2,1,0:T(1,128)}, u32[]{:S(2)}, u32[]{:S(2)}) collective-permute-start(f32[3,18,1,128]{3,2,1,0:T(1,128)} %get-tuple-element.223), channel_id=1, source_target_pairs={{4,0},{8,4},{12,8},{5,1},{9,5},{13,9},{6,2},{10,6},{14,10},{7,3},{... | collective-permute-start | bytes 82952 | tf_op jit(solution)/shard_map/ppermute | solution.py:23
  297.4 36.7 %collective-permute-start.26 = (f32[3,18,1,128]{3,2,1,0:T(1,128)}, f32[3,18,1,128]{3,2,1,0:T(1,128)}, u32[]{:S(2)}, u32[]{:S(2)}) collective-permute-start(f32[3,18,1,128]{3,2,1,0:T(1,128)} %get-tuple-element.221), channel_id=1, source_target_pairs={{4,0},{8,4},{12,8},{5,1},{9,5},{13,9},{6,2},{10,6},{14,10},{7,3},{... | collective-permute-start | bytes 82952 | tf_op jit(solution)/shard_map/ppermute | solution.py:23
  366.1 73.0 %collective-permute-start.32 = (f32[3,18,1,128]{3,2,1,0:T(1,128)}, f32[3,18,1,128]{3,2,1,0:T(1,128)}, u32[]{:S(2)}, u32[]{:S(2)}) collective-permute-start(f32[3,18,1,128]{3,2,1,0:T(1,128)} %get-tuple-element.219), channel_id=1, source_target_pairs={{4,0},{8,4},{12,8},{5,1},{9,5},{13,9},{6,2},{10,6},{14,10},{7,3},{... | collective-permute-start | bytes 82952 | tf_op jit(solution)/shard_map/ppermute | solution.py:23
  367.4 71.7 %collective-permute-start.33 = (f32[3,18,1,128]{3,2,1,0:T(1,128)}, f32[3,18,1,128]{3,2,1,0:T(1,128)}, u32[]{:S(2)}, u32[]{:S(2)}) collective-permute-start(f32[3,18,1,128]{3,2,1,0:T(1,128)} %get-tuple-element.218), channel_id=1, source_target_pairs={{0,4},{4,8},{8,12},{1,5},{5,9},{9,13},{2,6},{6,10},{10,14},{3,7},{... | collective-permute-start | bytes 82952 | tf_op jit(solution)/shard_map/ppermute | solution.py:20
  481.7 39.2 %collective-permute-start.38 = (f32[3,18,1,128]{3,2,1,0:T(1,128)}, f32[3,18,1,128]{3,2,1,0:T(1,128)}, u32[]{:S(2)}, u32[]{:S(2)}) collective-permute-start(f32[3,18,1,128]{3,2,1,0:T(1,128)} %get-tuple-element.217), channel_id=1, source_target_pairs={{4,0},{8,4},{12,8},{5,1},{9,5},{13,9},{6,2},{10,6},{14,10},{7,3},{... | collective-permute-start | bytes 82952 | tf_op jit(solution)/shard_map/ppermute | solution.py:23
  483.0 37.9 %collective-permute-start.39 = (f32[3,18,1,128]{3,2,1,0:T(1,128)}, f32[3,18,1,128]{3,2,1,0:T(1,128)}, u32[]{:S(2)}, u32[]{:S(2)}) collective-permute-start(f32[3,18,1,128]{3,2,1,0:T(1,128)} %get-tuple-element.216), channel_id=1, source_target_pairs={{0,4},{4,8},{8,12},{1,5},{5,9},{9,13},{2,6},{6,10},{10,14},{3,7},{... | collective-permute-start | bytes 82952 | tf_op jit(solution)/shard_map/ppermute | solution.py:20
  553.1 36.8 %collective-permute-start.44 = (f32[3,18,1,128]{3,2,1,0:T(1,128)S(1)}, f32[3,18,1,128]{3,2,1,0:T(1,128)S(1)}, u32[]{:S(2)}, u32[]{:S(2)}) collective-permute-start(f32[3,18,1,128]{3,2,1,0:T(1,128)S(1)} %get-tuple-element.215), channel_id=1, source_target_pairs={{4,0},{8,4},{12,8},{5,1},{9,5},{13,9},{6,2},{10,6},{14,10},{7,3},{... | collective-permute-start | bytes 82952 | tf_op jit(solution)/shard_map/ppermute | solution.py:23
  554.4 35.5 %collective-permute-start.45 = (f32[3,18,1,128]{3,2,1,0:T(1,128)S(1)}, f32[3,18,1,128]{3,2,1,0:T(1,128)S(1)}, u32[]{:S(2)}, u32[]{:S(2)}) collective-permute-start(f32[3,18,1,128]{3,2,1,0:T(1,128)S(1)} %get-tuple-element.214), channel_id=1, source_target_pairs={{0,4},{4,8},{8,12},{1,5},{5,9},{9,13},{2,6},{6,10},{10,14},{3,7},{... | collective-permute-start | bytes 82952 | tf_op jit(solution)/shard_map/ppermute | solution.py:20
  636.1 41.3 %collective-permute-start.50 = (f32[3,18,1,128]{3,2,1,0:T(1,128)}, f32[3,18,1,128]{3,2,1,0:T(1,128)S(1)}, u32[]{:S(2)}, u32[]{:S(2)}) collective-permute-start(f32[3,18,1,128]{3,2,1,0:T(1,128)} %get-tuple-element.213), channel_id=1, source_target_pairs={{4,0},{8,4},{12,8},{5,1},{9,5},{13,9},{6,2},{10,6},{14,10},{7,3},{... | collective-permute-start | bytes 82952 | tf_op jit(solution)/shard_map/ppermute | solution.py:23
  637.4 40.1 %collective-permute-start.51 = (f32[3,18,1,128]{3,2,1,0:T(1,128)}, f32[3,18,1,128]{3,2,1,0:T(1,128)S(1)}, u32[]{:S(2)}, u32[]{:S(2)}) collective-permute-start(f32[3,18,1,128]{3,2,1,0:T(1,128)} %get-tuple-element.212), channel_id=1, source_target_pairs={{0,4},{4,8},{8,12},{1,5},{5,9},{9,13},{2,6},{6,10},{10,14},{3,7},{... | collective-permute-start | bytes 82952 | tf_op jit(solution)/shard_map/ppermute | solution.py:20
  642.7 61.4 %collective-permute-start.68 = (f32[3,18,1,128]{3,2,1,0:T(1,128)}, f32[3,18,1,128]{3,2,1,0:T(1,128)S(1)}, u32[]{:S(2)}, u32[]{:S(2)}) collective-permute-start(f32[3,18,1,128]{3,2,1,0:T(1,128)} %get-tuple-element.201), channel_id=1, source_target_pairs={{4,0},{8,4},{12,8},{5,1},{9,5},{13,9},{6,2},{10,6},{14,10},{7,3},{... | collective-permute-start | bytes 82952 | tf_op jit(solution)/shard_map/ppermute | solution.py:23
  644.0 60.2 %collective-permute-start.69 = (f32[3,18,1,128]{3,2,1,0:T(1,128)}, f32[3,18,1,128]{3,2,1,0:T(1,128)}, u32[]{:S(2)}, u32[]{:S(2)}) collective-permute-start(f32[3,18,1,128]{3,2,1,0:T(1,128)} %get-tuple-element.200), channel_id=1, source_target_pairs={{0,4},{4,8},{8,12},{1,5},{5,9},{9,13},{2,6},{6,10},{10,14},{3,7},{... | collective-permute-start | bytes 82952 | tf_op jit(solution)/shard_map/ppermute | solution.py:20
  705.5 41.0 %collective-permute-start.56 = (f32[3,18,1,128]{3,2,1,0:T(1,128)S(1)}, f32[3,18,1,128]{3,2,1,0:T(1,128)S(1)}, u32[]{:S(2)}, u32[]{:S(2)}) collective-permute-start(f32[3,18,1,128]{3,2,1,0:T(1,128)S(1)} %get-tuple-element.211), channel_id=1, source_target_pairs={{4,0},{8,4},{12,8},{5,1},{9,5},{13,9},{6,2},{10,6},{14,10},{7,3},{... | collective-permute-start | bytes 82952 | tf_op jit(solution)/shard_map/ppermute | solution.py:23
  706.8 39.7 %collective-permute-start.57 = (f32[3,18,1,128]{3,2,1,0:T(1,128)S(1)}, f32[3,18,1,128]{3,2,1,0:T(1,128)S(1)}, u32[]{:S(2)}, u32[]{:S(2)}) collective-permute-start(f32[3,18,1,128]{3,2,1,0:T(1,128)S(1)} %get-tuple-element.210), channel_id=1, source_target_pairs={{0,4},{4,8},{8,12},{1,5},{5,9},{9,13},{2,6},{6,10},{10,14},{3,7},{... | collective-permute-start | bytes 82952 | tf_op jit(solution)/shard_map/ppermute | solution.py:20
  712.5 72.0 %collective-permute-start.70 = (f32[3,18,10,1]{3,2,1,0:T(8,128)}, f32[3,18,10,1]{3,2,1,0:T(8,128)}, u32[]{:S(2)}, u32[]{:S(2)}) collective-permute-start(f32[3,18,10,1]{3,2,1,0:T(8,128)} %get-tuple-element.157), channel_id=1, source_target_pairs={{1,0},{2,1},{3,2},{5,4},{6,5},{7,6},{9,8},{10,9},{11,10},{13,12},{... | collective-permute-start | bytes 6488 | tf_op jit(solution)/shard_map/ppermute | solution.py:23
  713.8 70.7 %collective-permute-start.71 = (f32[3,18,10,1]{3,2,1,0:T(8,128)}, f32[3,18,10,1]{3,2,1,0:T(8,128)}, u32[]{:S(2)}, u32[]{:S(2)}) collective-permute-start(f32[3,18,10,1]{3,2,1,0:T(8,128)} %get-tuple-element.156), channel_id=1, source_target_pairs={{0,1},{1,2},{2,3},{4,5},{5,6},{6,7},{8,9},{9,10},{10,11},{12,13},{... | collective-permute-start | bytes 6488 | tf_op jit(solution)/shard_map/ppermute | solution.py:20
  777.9 38.8 %collective-permute-start.62 = (f32[3,18,1,128]{3,2,1,0:T(1,128)}, f32[3,18,1,128]{3,2,1,0:T(1,128)}, u32[]{:S(2)}, u32[]{:S(2)}) collective-permute-start(f32[3,18,1,128]{3,2,1,0:T(1,128)} %get-tuple-element.209), channel_id=1, source_target_pairs={{4,0},{8,4},{12,8},{5,1},{9,5},{13,9},{6,2},{10,6},{14,10},{7,3},{... | collective-permute-start | bytes 82952 | tf_op jit(solution)/shard_map/ppermute | solution.py:23
  779.4 37.4 %collective-permute-start.63 = (f32[3,18,1,128]{3,2,1,0:T(1,128)}, f32[3,18,1,128]{3,2,1,0:T(1,128)}, u32[]{:S(2)}, u32[]{:S(2)}) collective-permute-start(f32[3,18,1,128]{3,2,1,0:T(1,128)} %get-tuple-element.208), channel_id=1, source_target_pairs={{0,4},{4,8},{8,12},{1,5},{5,9},{9,13},{2,6},{6,10},{10,14},{3,7},{... | collective-permute-start | bytes 82952 | tf_op jit(solution)/shard_map/ppermute | solution.py:20
  816.7 213.6 %reduce-scatter.2.cloned.1.call-start = ((), (), s32[]{:S(2)}) async-start(), calls=%async_computation.12 | async-start | bytes 540672 | tf_op jit(solution)/shard_map/reduce_scatter | solution.py:284
  (209 other events, 2557.2 us)
Sparse Core Ops, SparseCore 0:
  888.7 141.5 reduce-scatter.1
where the time goes:
time: 1060 us; the launch traced here: 1040 us
  starting transfers between devices  321 us (30%)
  local copies, waits for them, and re-layouts  285 us (27%)
  other arithmetic  245 us (23%)
  waiting for transfers between devices  161 us (15%)
  between operations  17.9 us (2%)
    ppermute x39, starting transfers between devices, extended_2(): lax.ppermute(lax.slice_in_dim(block, block.shape[dim] - width, None, axis...  169 us
    reduce_scatter x1, waiting for transfers between devices, local(): lax.psum_scatter(region_partial, ('gx', 'gy', 'gz'), scatter_dimension=1,...  141 us
    gather x20, local copies, waits for them, and re-layouts, fault_sum(): own_values = flattened[:, cell_index]  131 us
    scatter-add x10, other arithmetic, fault_sum(): faults = jnp.zeros((flattened.shape[1],), jnp.float32).at[cell_index.resh...  118 us
    all_to_all x10, starting transfers between devices, fault_exchange(): lax.all_to_all(values, ('gy', 'gz'), split_axis=1, concat_axis=1, tiled=T...  95.3 us
    reshape x10, local copies, waits for them, and re-layouts, fault_sum(): flattened = lagrange.reshape(lagrange.shape[0], -1)  53.4 us
    ppermute x39, starting transfers between devices, extended_2(): lax.ppermute(lax.slice_in_dim(block, 0, width, axis=dim), axis, backward)  51.1 us
  transfers between devices with their start and end apart: 90, of which 18 were waited for; matrix products, arithmetic and copies ran while one was open for 35% of the time, Pallas kernels for 0%

commit v1 on v0

v1 whole, which is shorter than its diff:
```python
import functools

import jax
import jax.numpy as jnp
from jax import lax
from jax.experimental import pallas as pl
from jax.experimental.pallas import tpu as pltpu
from jax.sharding import PartitionSpec as P

ITERS = 6
BOX = 4
PARAM_REGIONS = 32
MESH = pl.DeviceIdType.MESH
HIGHEST = lax.Precision.HIGHEST

fluid_viscosity = (0.4, 0.5, 1.0)
sigma_sq = 64.0


def phase_mobility(water_sat, oil_sat):
    gas_sat = 1.0 - water_sat - oil_sat
    return [
        water_sat * water_sat / fluid_viscosity[0],
        oil_sat * oil_sat / fluid_viscosity[1],
        gas_sat * gas_sat / fluid_viscosity[2],
    ]


def mobility_slopes(water_sat, oil_sat):
    gas_sat = 1.0 - water_sat - oil_sat
    return (
        2.0 * water_sat / fluid_viscosity[0] - 2.0 * gas_sat / fluid_viscosity[2],
        2.0 * oil_sat / fluid_viscosity[1] - 2.0 * gas_sat / fluid_viscosity[2],
    )


def split_bf16(value):
    high = value.astype(jnp.bfloat16)
    return high, (value - high.astype(jnp.float32)).astype(jnp.bfloat16)


def kernel(
    counts,
    pressure_ref,
    saturation_ref,
    perm_ref,
    porosity_ref,
    flags_ref,
    inverse_ref,
    seismic_ref,
    well_rows_ref,
    well_cols_ref,
    well_top_ref,
    well_len_ref,
    bhp_ref,
    obs_ref,
    fault_row_ref,
    fault_z_ref,
    fault_trans_ref,
    fault_up_ref,
    fault_live_ref,
    lam_ref,
    box_ref,
    wp,
    wm,
    src,
    explicit,
    row_hot,
    z_hot,
    fault_coef,
    bx_s,
    by_s,
    bz_s,
    bx_r,
    by_r,
    bz_r,
    b_ss,
    b_rs,
    m_s,
    m_r,
    m_ss,
    m_rs,
    w_s,
    w_r,
    w_ss,
    w_rs,
    x_s,
    y_s,
    z_s,
    x_r,
    y_r,
    z_r,
    f_ss,
    f_rs,
    c_s,
    c_r,
    c_ss,
    c_rs,
):
    n_gx, n_gy, n_gz = counts
    here = (lax.axis_index("gx"), lax.axis_index("gy"), lax.axis_index("gz"))
    peers = n_gy * n_gz
    me = here[1] * n_gz + here[2]
    shape = perm_ref.shape
    nx, ny, nz = shape
    rows = nx * ny
    slots = m_r.shape[2]
    wide = peers * slots

    def toward(dim, step):
        moved = list(here)
        moved[dim] = lax.rem(here[dim] + step + counts[dim], counts[dim])
        return tuple(moved)

    def peer(offset):
        other = lax.rem(me + offset, peers)
        return (here[0], other // n_gz, lax.rem(other, n_gz))

    def remote(source, target, send, recv, device):
        return pltpu.make_async_remote_copy(
            src_ref=source,
            dst_ref=target,
            send_sem=send,
            recv_sem=recv,
            device_id=device,
            device_id_type=MESH,
        )

    m_r[...] = jnp.zeros_like(m_r)
    c_r[...] = jnp.zeros_like(c_r)

    barrier = pltpu.get_barrier_semaphore()
    for offset in range(1, peers):
        pl.semaphore_signal(barrier, inc=1, device_id=peer(offset), device_id_type=MESH)
    for step in (1, -1):
        pl.semaphore_signal(barrier, inc=1, device_id=toward(0, step), device_id_type=MESH)
    pl.semaphore_wait(barrier, peers + 1)

    xi = lax.broadcasted_iota(jnp.int32, shape, 0)
    yi = lax.broadcasted_iota(jnp.int32, shape, 1)
    zi = lax.broadcasted_iota(jnp.int32, shape, 2)
    iotas = (xi, yi, zi)
    diagonal = xi == zi

    def pack(column):
        return jnp.sum(jnp.where(diagonal, column, 0.0), axis=0)

    def unpack(tile):
        return jnp.sum(jnp.where(diagonal, tile[None], 0.0), axis=2, keepdims=True)

    def ahead(field, dim, halo):
        if dim == 0:
            return jnp.concatenate([field[1:], halo[None]], axis=0)
        last = shape[dim] - 1
        edge = halo if dim == 1 else unpack(halo)
        return jnp.where(iotas[dim] == last, edge, pltpu.roll(field, last, dim))

    def behind(field, dim, halo):
        if dim == 0:
            return jnp.concatenate([halo[None], field[:-1]], axis=0)
        edge = halo if dim == 1 else unpack(halo)
        return jnp.where(iotas[dim] == 0, edge, pltpu.roll(field, 1, dim))

    perm = perm_ref[...]
    flags = flags_ref[...].astype(jnp.float32)
    pressure = [pressure_ref[t] for t in range(2)]
    mobility = [
        phase_mobility(saturation_ref[t + 1, 0], saturation_ref[t + 1, 1]) for t in range(2)
    ]
    bundle = [perm] + mobility[0] + mobility[1] + [flags] + pressure
    for q, field in enumerate(bundle):
        bx_s[0, q] = field[nx - 1]
        bx_s[1, q] = field[0]
        by_s[0, q] = field[:, ny - 1 :, :]
        by_s[1, q] = field[:, :1, :]
        bz_s[0, q] = pack(field[:, :, nz - 1 :])
        bz_s[1, q] = pack(field[:, :, :1])
    b_copies = []
    for dim, (sent, got) in enumerate(((bx_s, bx_r), (by_s, by_r), (bz_s, bz_r))):
        for side, step in ((0, 1), (1, -1)):
            copy = remote(
                sent.at[side],
                got.at[side],
                b_ss.at[dim, side],
                b_rs.at[dim, side],
                toward(dim, step),
            )
            copy.start()
            b_copies.append(copy)

    fault_z = fault_z_ref[...]
    hot = (lax.broadcasted_iota(jnp.int32, (rows, wide), 0) == fault_row_ref[...]).astype(
        jnp.float32
    ).astype(jnp.bfloat16)
    row_hot[:rows] = hot
    row_hot[rows:] = hot
    z_hot[...] = (
        (lax.broadcasted_iota(jnp.int32, (nz, wide), 0) == fault_z)
        .astype(jnp.float32)
        .astype(jnp.bfloat16)
    )

    def gather(fields):
        stacked = []
        for field in fields:
            stacked.append(
                jnp.concatenate(split_bf16(field.reshape(rows, nz).T), axis=1)
            )
        columns = jnp.dot(
            jnp.concatenate(stacked, axis=0), row_hot[...], preferred_element_type=jnp.float32
        )
        chosen = lax.broadcasted_iota(jnp.int32, (nz, wide), 0) == fault_z
        return [
            jnp.sum(
                jnp.where(chosen, columns[k * nz : (k + 1) * nz], 0.0), axis=0, keepdims=True
            )
            for k in range(len(fields))
        ]

    own = gather(mobility[0]) + gather(mobility[1])
    for p in range(peers):
        for q in range(6):
            m_s[p, q : q + 1, :] = own[q][:, p * slots : (p + 1) * slots]
        m_s[p, 6:8, :] = jnp.zeros((2, slots), jnp.float32)
    m_copies = []
    for offset in range(1, peers):
        other = lax.rem(me + offset, peers)
        copy = remote(
            m_s.at[other], m_r.at[me], m_ss.at[offset], m_rs.at[offset], peer(offset)
        )
        copy.start()
        m_copies.append(copy)

    n_wells = well_top_ref.shape[0]
    well_hot = (
        lax.broadcasted_iota(jnp.int32, (n_wells, rows), 1) == well_rows_ref[...]
    ).astype(jnp.float32)
    well_hot_t = (
        lax.broadcasted_iota(jnp.int32, (rows, n_wells), 0) == well_cols_ref[...]
    ).astype(jnp.float32)
    depth = here[2] * nz + lax.broadcasted_iota(jnp.int32, (n_wells, nz), 1)
    top = well_top_ref[...]
    perforated = ((depth >= top) & (depth < top + well_len_ref[...])).astype(jnp.float32)
    total = [perm * (mobility[t][0] + mobility[t][1] + mobility[t][2]) for t in range(2)]
    lane = lax.broadcasted_iota(jnp.int32, (n_wells, nz), 1)
    rates = jnp.zeros((n_wells, nz), jnp.float32)
    for t in range(2):
        with_pressure = jnp.dot(
            well_hot,
            (total[t] * pressure[t]).reshape(rows, nz),
            precision=HIGHEST,
            preferred_element_type=jnp.float32,
        )
        without = jnp.dot(
            well_hot,
            total[t].reshape(rows, nz),
            precision=HIGHEST,
            preferred_element_type=jnp.float32,
        )
        rate = jnp.sum(
            perforated * (with_pressure - bhp_ref[t] * without), axis=1, keepdims=True
        )
        rates = jnp.where(lane == t, rate, rates)
    w_s[...] = rates
    w_copies = []
    for offset in range(1, n_gz):
        copy = remote(
            w_s, w_r.at[offset], w_ss.at[offset], w_rs.at[offset], toward(2, offset)
        )
        copy.start()
        w_copies.append(copy)

    for copy in b_copies:
        copy.wait()
    halos = ((bx_r, bx_s), (by_r, by_s), (bz_r, bz_s))
    for dim in range(3):
        got = halos[dim][0]
        up_ok = (here[dim] < counts[dim] - 1).astype(jnp.float32)
        low_ok = (here[dim] > 0).astype(jnp.float32)
        up_face = jnp.sqrt(perm * ahead(perm, dim, got[1, 0]))
        up_face = up_face * jnp.where(iotas[dim] == shape[dim] - 1, up_ok, 1.0)
        low_face = jnp.sqrt(perm * behind(perm, dim, got[0, 0]))
        low_face = low_face * jnp.where(iotas[dim] == 0, low_ok, 1.0)
        own_flags = flags.astype(jnp.int32)
        low_flags = behind(flags, dim, got[0, 7]).astype(jnp.int32)
        for t in range(2):
            bit = 3 * t + dim
            own_up = jnp.bitwise_and(jnp.right_shift(own_flags, bit), 1) == 1
            low_up = jnp.bitwise_and(jnp.right_shift(low_flags, bit), 1) == 1
            for k in range(3):
                q = 1 + 3 * t + k
                m = mobility[t][k]
                wp[t, dim, k] = up_face * jnp.where(own_up, m, ahead(m, dim, got[1, q]))
                wm[t, dim, k] = low_face * jnp.where(low_up, behind(m, dim, got[0, q]), m)

    for copy in m_copies:
        copy.wait()
    for t in range(2):
        own_up = jnp.bitwise_and(jnp.right_shift(fault_up_ref[...], t), 1) == 1
        scale = fault_trans_ref[...] * fault_live_ref[...]
        for k in range(3):
            q = 3 * t + k
            other = jnp.concatenate([m_r[p, q : q + 1, :] for p in range(peers)], axis=1)
            fault_coef[q : q + 1, :] = scale * jnp.where(own_up, own[q], other)

    for copy in w_copies:
        copy.wait()
    rates = w_s[...]
    for offset in range(1, n_gz):
        rates = rates + w_r[offset]
    explicit_sum = jnp.zeros(shape, jnp.float32)
    for t in range(2):
        misfit = (rates[:, t : t + 1] - obs_ref[t]) / sigma_sq
        weight = misfit * perforated
        spread = jnp.dot(
            well_hot_t, weight, precision=HIGHEST, preferred_element_type=jnp.float32
        ).reshape(shape)
        spread_bhp = jnp.dot(
            well_hot_t, weight * bhp_ref[t], precision=HIGHEST, preferred_element_type=jnp.float32
        ).reshape(shape)
        drawn = pressure[t] * spread - spread_bhp
        water_slope, oil_slope = mobility_slopes(
            saturation_ref[t + 1, 0], saturation_ref[t + 1, 1]
        )
        src[t, 0] = total[t] * spread
        water_source = perm * drawn * water_slope
        if t == 1:
            water_source = water_source + saturation_ref[2, 0] - seismic_ref[...]
        src[t, 1] = water_source
        src[t, 2] = perm * drawn * oil_slope
        explicit_sum = explicit_sum + total[t] * drawn
    explicit[...] = explicit_sum

    def relax(t, coupling):
        residual = [src[t, u] for u in range(3)]
        if coupling is not None:
            residual[0] = residual[0] + coupling
        for k in range(3):
            lam_ref[t, k] = (
                inverse_ref[t, 0, k] * residual[0]
                + inverse_ref[t, 1, k] * residual[1]
                + inverse_ref[t, 2, k] * residual[2]
            )

    def face_copies(slot):
        made = []
        for dim, (sent, got) in enumerate(((x_s, x_r), (y_s, y_r), (z_s, z_r))):
            for side, step in ((0, 1), (1, -1)):
                made.append(
                    remote(
                        sent.at[side],
                        got.at[slot, side],
                        f_ss.at[dim, side],
                        f_rs.at[slot, dim, side],
                        toward(dim, step),
                    )
                )
        return made

    def products(t):
        lam = [lam_ref[t, k] for k in range(3)]
        up = []
        down = []
        for dim in range(3):
            up.append(sum(wp[t, dim, k] * lam[k] for k in range(3)))
            down.append(sum(wm[t, dim, k] * lam[k] for k in range(3)))
        x_s[0] = up[0][nx - 1]
        x_s[1] = down[0][0]
        y_s[0] = up[1][:, ny - 1 :, :]
        y_s[1] = down[1][:, :1, :]
        z_s[0] = pack(up[2][:, :, nz - 1 :])
        z_s[1] = pack(down[2][:, :, :1])
        return lam, up, down

    def terms(up, down, slot):
        faces = (x_r, y_r, z_r)
        upper = [ahead(down[dim], dim, faces[dim][slot, 1]) for dim in range(3)]
        lower = [behind(up[dim], dim, faces[dim][slot, 0]) for dim in range(3)]
        return upper, lower

    def sweep(t, n_face, n_fault):
        face_slot = lax.rem(n_face, 2)
        slot = lax.rem(n_fault, 2)
        lam, up, down = products(t)
        faces = face_copies(face_slot)
        for copy in faces:
            copy.start()
        values = gather(lam)
        sent = sum(
            fault_coef[3 * t + k : 3 * t + k + 1, :] * values[k] for k in range(3)
        )
        for p in range(peers):
            c_s[p] = sent[:, p * slots : (p + 1) * slots]
        copies = []
        for offset in range(1, peers):
            other = lax.rem(me + offset, peers)
            copy = remote(
                c_s.at[other],
                c_r.at[slot, me],
                c_ss.at[offset],
                c_rs.at[slot, offset],
                peer(offset),
            )
            copy.start()
            copies.append(copy)
        for copy in faces:
            copy.wait()
        upper, lower = terms(up, down, face_slot)
        coupling = upper[0] + lower[0] + upper[1] + lower[1] + upper[2] + lower[2]
        for copy in copies:
            copy.wait()
        arrived = jnp.concatenate([c_r[slot, p] for p in range(peers)], axis=1)
        picked = jnp.where(
            lax.broadcasted_iota(jnp.int32, (rows, wide), 0) == fault_row_ref[...], arrived, 0.0
        )
        both = jnp.concatenate(split_bf16(picked), axis=0)
        added = lax.dot_general(
            both,
            z_hot[...],
            (((1,), (1,)), ((), ())),
            preferred_element_type=jnp.float32,
        )
        coupling = coupling + (added[:rows] + added[rows:]).reshape(shape)
        relax(t, coupling)

    log_perm = explicit_sum
    for turn, t in enumerate((1, 0)):
        if t == 0:
            porosity = porosity_ref[...]
            src[0, 1] += porosity * (lam_ref[1, 0] - lam_ref[1, 2])
            src[0, 2] += porosity * (lam_ref[1, 1] - lam_ref[1, 2])
        relax(t, None)

        def body(step, carry, t=t, turn=turn):
            sweep(t, turn * ITERS + step, turn * (ITERS - 1) + step)
            return carry

        lax.fori_loop(0, ITERS - 1, body, 0)
        slot = (turn * ITERS + ITERS - 1) % 2
        lam, up, down = products(t)
        faces = face_copies(slot)
        for copy in faces:
            copy.start()
        for copy in faces:
            copy.wait()
        upper, lower = terms(up, down, slot)
        p_here = pressure_ref[t]
        flux = jnp.zeros(shape, jnp.float32)
        for dim in range(3):
            got = halos[dim][0]
            flux = (
                flux
                + 0.5
                * (p_here - ahead(p_here, dim, got[1, 8 + t]))
                * (up[dim] - upper[dim])
                + 0.5
                * (behind(p_here, dim, got[0, 8 + t]) - p_here)
                * (lower[dim] - down[dim])
            )
        explicit[...] -= flux

    porosity_sum = jnp.zeros(shape, jnp.float32)
    for t in range(2):
        water = saturation_ref[t + 1, 0] - saturation_ref[t, 0]
        oil = saturation_ref[t + 1, 1] - saturation_ref[t, 1]
        porosity_sum = porosity_sum + (
            lam_ref[t, 0] * water + lam_ref[t, 1] * oil - lam_ref[t, 2] * (water + oil)
        )
    z_boxes = (
        lax.broadcasted_iota(jnp.int32, (nz, nz), 0) // BOX
        == lax.broadcasted_iota(jnp.int32, (nz, nz), 1)
    ).astype(jnp.float32)
    for q, field in enumerate((explicit[...], -porosity_sum)):
        in_x = jnp.sum(field.reshape(nx // BOX, BOX, ny, nz), axis=1)
        box_ref[q] = jnp.dot(
            in_x.reshape(nx // BOX * ny, nz),
            z_boxes,
            precision=HIGHEST,
            preferred_element_type=jnp.float32,
        )


def local(
    pressure,
    saturation,
    permeability,
    porosity,
    upwind_flags,
    diag_inverse,
    seismic_obs,
    well_x,
    well_y,
    well_top,
    well_len,
    well_bhp,
    well_obs,
    fault_cell,
    fault_count,
    fault_trans,
    fault_up,
    region_map,
):
    counts = tuple(lax.axis_size(axis) for axis in ("gx", "gy", "gz"))
    nx, ny, nz = permeability.shape
    peers, slots = fault_cell.shape[1:]
    wide = peers * slots
    n_wells = well_x.shape[2]
    well_row = well_x[0, 0] * ny + well_y[0, 0]
    cells = fault_cell[0]
    live = (
        jnp.arange(slots, dtype=jnp.int32)[None, :] < fault_count[0][:, None]
    ).astype(jnp.float32)
    vmem = pl.BlockSpec(memory_space=pltpu.VMEM)
    f32 = jnp.float32
    dma = pltpu.SemaphoreType.DMA
    faces = [(2, ny, nz), (2, nx, 1, nz), (2, ny, nz)]
    bundles = [(2, 10, ny, nz), (2, 10, nx, 1, nz), (2, 10, ny, nz)]
    scratch = [
        pltpu.VMEM((2, 3, 3, nx, ny, nz), f32),
        pltpu.VMEM((2, 3, 3, nx, ny, nz), f32),
        pltpu.VMEM((2, 3, nx, ny, nz), f32),
        pltpu.VMEM((nx, ny, nz), f32),
        pltpu.VMEM((2 * nx * ny, wide), jnp.bfloat16),
        pltpu.VMEM((nz, wide), jnp.bfloat16),
        pltpu.VMEM((8, wide), f32),
        *[pltpu.VMEM(s, f32) for s in bundles],
        *[pltpu.VMEM(s, f32) for s in bundles],
        dma((3, 2)),
        dma((3, 2)),
        pltpu.VMEM((peers, 8, slots), f32),
        pltpu.VMEM((peers, 8, slots), f32),
        dma((peers,)),
        dma((peers,)),
        pltpu.VMEM((n_wells, nz), f32),
        pltpu.VMEM((counts[2], n_wells, nz), f32),
        dma((counts[2],)),
        dma((counts[2],)),
        *[pltpu.VMEM(s, f32) for s in faces],
        *[pltpu.VMEM((2,) + s, f32) for s in faces],
        dma((3, 2)),
        dma((2, 3, 2)),
        pltpu.VMEM((peers, 1, slots), f32),
        pltpu.VMEM((2, peers, 1, slots), f32),
        dma((peers,)),
        dma((2, peers)),
    ]
    adjoint, boxes = pl.pallas_call(
        functools.partial(kernel, counts),
        out_shape=(
            jax.ShapeDtypeStruct((2, 3, nx, ny, nz), f32),
            jax.ShapeDtypeStruct((2, nx // BOX * ny, nz), f32),
        ),
        in_specs=[vmem] * 18,
        out_specs=(vmem, vmem),
        scratch_shapes=scratch,
        compiler_params=pltpu.CompilerParams(
            collective_id=0, has_side_effects=True, vmem_limit_bytes=48 * 2**20
        ),
    )(
        pressure,
        saturation,
        permeability,
        porosity,
        upwind_flags,
        diag_inverse,
        seismic_obs,
        well_row[:, None],
        well_row[None, :],
        well_top[0, 0][:, None],
        well_len[0, 0][:, None],
        well_bhp[:, 0, 0][:, :, None],
        well_obs[:, 0, 0][:, :, None],
        (cells // nz).reshape(1, wide),
        (cells % nz).reshape(1, wide),
        fault_trans[0].reshape(1, wide),
        fault_up[0].reshape(1, wide),
        live.reshape(1, wide),
    )
    box_totals = boxes[:, :, : nz // BOX].reshape(2, nx // BOX, ny // BOX, BOX, nz // BOX)
    box_totals = jnp.sum(box_totals, axis=3).reshape(2, -1)
    region_labels = PARAM_REGIONS * counts[0] * counts[1] * counts[2]
    chosen = (
        region_map.reshape(-1)[:, None] == jnp.arange(region_labels, dtype=jnp.int32)[None, :]
    ).astype(f32)
    region_partial = jnp.dot(box_totals, chosen, precision=HIGHEST)
    region_grad = lax.psum_scatter(
        region_partial, ("gx", "gy", "gz"), scatter_dimension=1, tiled=True
    )
    return (adjoint, region_grad)


def solution(mesh):
    placed = (
        P(None, "gx", "gy", "gz"),
        P(None, None, "gx", "gy", "gz"),
        P("gx", "gy", "gz"),
        P("gx", "gy", "gz"),
        P("gx", "gy", "gz"),
        P(None, None, None, "gx", "gy", "gz"),
        P("gx", "gy", "gz"),
        P("gx", "gy", None),
        P("gx", "gy", None),
        P("gx", "gy", None),
        P("gx", "gy", None),
        P(None, "gx", "gy", None),
        P(None, "gx", "gy", None),
        P(("gx", "gy", "gz"), None, None),
        P(("gx", "gy", "gz"), None),
        P(("gx", "gy", "gz"), None, None),
        P(("gx", "gy", "gz"), None, None),
        P("gx", "gy", "gz"),
    )
    return jax.shard_map(
        local,
        mesh=mesh,
        in_specs=placed,
        out_specs=(P(None, None, "gx", "gy", "gz"), P(None, ("gx", "gy", "gz"))),
        check_vma=False,
    )
```

time: 1060 us -> 244 us (0.23); the launches traced: 1040 us -> 243 us
  starting transfers between devices: 321 us -> 0.04 us
  local copies, waits for them, and re-layouts: 285 us -> 14 us
  other arithmetic: 245 us -> 2.9 us
  Pallas kernels: 0 us -> 76.4 us
  waiting for transfers between devices: 161 us -> 133 us
    ppermute x78 -> x0, starting transfers between devices: 220 us -> none  [the longest x39 169 us: extended_2(): lax.ppermute(lax.slice_in_dim(block, block.shape[dim] - width, None, axis...]
    gather x31 -> x0, local copies, waits for them, and re-layouts: 151 us -> none  [the longest x20 131 us: fault_sum(): own_values = flattened[:, cell_index]]
    scatter-add x15 -> x0, other arithmetic: 145 us -> none  [the longest x10 118 us: fault_sum(): faults = jnp.zeros((flattened.shape[1],), jnp.float32).at[cell_index.resh...]
    reduce_scatter x1 -> x0, waiting for transfers between devices: 141 us -> none  [local(): lax.psum_scatter(region_partial, ('gx', 'gy', 'gz'), scatter_dimension=1,...]
    unnamed x1 -> x2, waiting for transfers between devices: 0.02 us -> 133 us
    all_to_all x11 -> x0, starting transfers between devices: 101 us -> none  [the longest x10 95.3 us: fault_exchange(): lax.all_to_all(values, ('gy', 'gz'), split_axis=1, concat_axis=1, tiled=T...]
    pallas_call x0 -> x1, Pallas kernels: none -> 76.4 us  [local(): pl.pallas_call(functools.partial(kernel, counts), out_shape=(jax.ShapeDty...]
    reshape x11 -> x1, local copies, waits for them, and re-layouts: 56.9 us -> 0.09 us  [local(): box_totals = jnp.sum(box_totals, axis=3).reshape(2, -1)]
  transfers between devices with their start and end apart: 90 -> 1, of which waited for: 18 -> 1; matrix products, arithmetic and copies ran while one was open for 35% -> 0% of each run, Pallas kernels for 0% -> 0%
where the time goes in v1:
time: 244 us; the launch traced here: 243 us
  waiting for transfers between devices  133 us (55%)
  Pallas kernels  76.4 us (31%)
  between operations  14.1 us (6%)
  local copies, waits for them, and re-layouts  14 us (6%)
  other arithmetic  2.9 us (1%)
    unnamed x2, waiting for transfers between devices  133 us
    pallas_call x1, Pallas kernels, local(): pl.pallas_call(functools.partial(kernel, counts), out_shape=(jax.ShapeDty...  76.4 us
    unnamed x20, local copies, waits for them, and re-layouts  10 us
  transfers between devices with their start and end apart: 1, of which 1 were waited for; matrix products, arithmetic and copies ran while one was open for 0% of the time, Pallas kernels for 0%

profile of v1, /device:TPU:0, one launch (start us, length us, event | category | flops | bytes accessed | tf_op | source)
XLA Modules:
  0.0 242.8 jit_solution(1501006656448888227)
XLA Ops:
  7.2 0.8 eq.17
  8.0 0.7 fusion.1
  8.7 0.7 and_select_fusion
  9.4 0.7 and_select_fusion.1.fault_row_ref
  10.2 0.7 fusion.2
  10.8 0.1 copy.25.well_rows_ref
  10.9 0.7 copy.26.well_top_ref
  11.7 0.7 copy.27.well_len_ref
  12.4 0.8 copy.28.bhp_ref
  13.2 0.8 copy.29.obs_ref
  14.0 1.3 copy-done
  15.3 1.0 copy-done.1
  16.3 0.9 copy-done.2
  17.2 0.8 copy-done.3
  18.0 0.8 copy-done.4
  18.9 0.8 copy-done.5
  19.7 0.8 copy-done.6
  20.5 0.7 copy-done.7
  21.2 0.7 copy-done.8
  21.9 76.4 %shard_map.185 = (f32[2,3,16,8,128]{4,3,2,1,0:T(8,128)S(1)}, f32[2,32,128]{2,1,0:T(8,128)S(1)}) custom-call(f32[2,16,8,128]{3,2,1,0:T(8,128)S(1)} %copy-done.2, f32[3,2,16,8,128]{4,3,2,1,0:T(8,128)S(1)} %copy-done.1, f32[16,8,128]{2,1,0:T(8,128)S(1)} %copy-done.3, f32[16,8,128]{2,1,0:T(8,128)S(1)} %copy-done.4, s32[16,8,128]{2,1,0:T(8,128)S(1)} %copy-done.5, ...), custom_call_target="tpu_custom_call" | custom-call | tf_op jit(solution)/shard_map/pallas_call | solution.py:547
  98.5 1.9 convolution_bitcast_fusion
  100.4 133.5 %reduce-scatter.4.cloned.1.call-done = f32[32,2]{1,0:T(8,128)} async-done(((f32[1024,2]{1,0:T(8,128)}), f32[32,2]{1,0:T(8,128)}) %reduce-scatter.4.cloned.1.call-update) | async-done | bytes 272
  233.8 1.4 copy.31
  235.2 0.7 copy.33
  (13 shorter events, 0.2 us)
Async XLA Ops:
  7.2 226.7 %reduce-scatter.4.cloned.1.call-start = ((), (), s32[]{:S(2)}) async-start(), calls=%async_computation.1 | async-start | bytes 540672
  14.0 1.3 copy-start
  15.3 1.0 copy-start.1
  16.3 0.9 copy-start.2
  17.2 0.8 copy-start.3
  18.0 0.8 copy-start.4
  18.9 0.8 copy-start.5
  19.7 0.8 copy-start.6
  20.5 0.7 copy-start.7
  21.2 0.7 copy-start.8
Sparse Core Ops, SparseCore 0:
  100.5 133.3 reduce-scatter.3

commit v2 on v1

--- a/solution.py
+++ b/solution.py
@@ -41,6 +41,26 @@
 
 def kernel(
     counts,
+    pressure_hbm,
+    saturation_hbm,
+    perm_hbm,
+    porosity_hbm,
+    flags_hbm,
+    inverse_hbm,
+    seismic_hbm,
+    well_x_ref,
+    well_y_ref,
+    well_top_ref,
+    well_len_ref,
+    bhp_ref,
+    obs_ref,
+    fault_cell_ref,
+    fault_count_ref,
+    fault_trans_ref,
+    fault_up_ref,
+    map_ref,
+    lam_ref,
+    region_ref,
     pressure_ref,
     saturation_ref,
     perm_ref,
@@ -48,19 +68,7 @@
     flags_ref,
     inverse_ref,
     seismic_ref,
-    well_rows_ref,
-    well_cols_ref,
-    well_top_ref,
-    well_len_ref,
-    bhp_ref,
-    obs_ref,
-    fault_row_ref,
-    fault_z_ref,
-    fault_trans_ref,
-    fault_up_ref,
-    fault_live_ref,
-    lam_ref,
-    box_ref,
+    in_sem,
     wp,
     wm,
     src,
@@ -96,6 +104,14 @@
     c_r,
     c_ss,
     c_rs,
+    g_s,
+    g_r,
+    g_ss,
+    g_rs,
+    r_s,
+    r_r,
+    r_ss,
+    r_rs,
 ):
     n_gx, n_gy, n_gz = counts
     here = (lax.axis_index("gx"), lax.axis_index("gy"), lax.axis_index("gz"))
@@ -126,15 +142,33 @@
             device_id_type=MESH,
         )
 
+    loads = [
+        pltpu.make_async_copy(source, target, in_sem.at[n])
+        for n, (source, target) in enumerate(
+            (
+                (perm_hbm, perm_ref),
+                (saturation_hbm, saturation_ref),
+                (flags_hbm, flags_ref),
+                (pressure_hbm, pressure_ref),
+                (seismic_hbm, seismic_ref),
+                (inverse_hbm, inverse_ref),
+                (porosity_hbm, porosity_ref),
+            )
+        )
+    ]
+    for load in loads:
+        load.start()
     m_r[...] = jnp.zeros_like(m_r)
     c_r[...] = jnp.zeros_like(c_r)
 
     barrier = pltpu.get_barrier_semaphore()
     for offset in range(1, peers):
         pl.semaphore_signal(barrier, inc=1, device_id=peer(offset), device_id_type=MESH)
-    for step in (1, -1):
+    for step in range(1, n_gx):
         pl.semaphore_signal(barrier, inc=1, device_id=toward(0, step), device_id_type=MESH)
-    pl.semaphore_wait(barrier, peers + 1)
+    pl.semaphore_wait(barrier, peers - 1 + n_gx - 1)
+    for load in loads[:4]:
+        load.wait()
 
     xi = lax.broadcasted_iota(jnp.int32, shape, 0)
     yi = lax.broadcasted_iota(jnp.int32, shape, 1)
@@ -188,8 +222,13 @@
             copy.start()
             b_copies.append(copy)
 
-    fault_z = fault_z_ref[...]
-    hot = (lax.broadcasted_iota(jnp.int32, (rows, wide), 0) == fault_row_ref[...]).astype(
+    def as_row(ref):
+        return jnp.concatenate([ref[0, p : p + 1, :] for p in range(peers)], axis=1)
+
+    fault_cell = as_row(fault_cell_ref)
+    fault_row = fault_cell // nz
+    fault_z = fault_cell - fault_row * nz
+    hot = (lax.broadcasted_iota(jnp.int32, (rows, wide), 0) == fault_row).astype(
         jnp.float32
     ).astype(jnp.bfloat16)
     row_hot[:rows] = hot
@@ -231,16 +270,29 @@
         copy.start()
         m_copies.append(copy)
 
-    n_wells = well_top_ref.shape[0]
+    n_wells = well_top_ref.shape[2]
+    eye = lax.broadcasted_iota(jnp.int32, (n_wells, n_wells), 0) == lax.broadcasted_iota(
+        jnp.int32, (n_wells, n_wells), 1
+    )
+
+    def as_column(row):
+        return jnp.sum(jnp.where(eye, row.astype(jnp.float32), 0.0), axis=1, keepdims=True)
+
+    well_row = well_x_ref[0] * ny + well_y_ref[0]
+    bhp = [as_column(bhp_ref[t, 0]) for t in range(2)]
     well_hot = (
-        lax.broadcasted_iota(jnp.int32, (n_wells, rows), 1) == well_rows_ref[...]
+        lax.broadcasted_iota(jnp.int32, (n_wells, rows), 1).astype(jnp.float32)
+        == as_column(well_row)
     ).astype(jnp.float32)
     well_hot_t = (
-        lax.broadcasted_iota(jnp.int32, (rows, n_wells), 0) == well_cols_ref[...]
+        lax.broadcasted_iota(jnp.int32, (rows, n_wells), 0) == well_row
     ).astype(jnp.float32)
-    depth = here[2] * nz + lax.broadcasted_iota(jnp.int32, (n_wells, nz), 1)
-    top = well_top_ref[...]
-    perforated = ((depth >= top) & (depth < top + well_len_ref[...])).astype(jnp.float32)
+    depth = (here[2] * nz + lax.broadcasted_iota(jnp.int32, (n_wells, nz), 1)).astype(
+        jnp.float32
+    )
+    top = as_column(well_top_ref[0])
+    bottom = as_column(well_top_ref[0] + well_len_ref[0])
+    perforated = jnp.where((depth >= top) & (depth < bottom), 1.0, 0.0)
     total = [perm * (mobility[t][0] + mobility[t][1] + mobility[t][2]) for t in range(2)]
     lane = lax.broadcasted_iota(jnp.int32, (n_wells, nz), 1)
     rates = jnp.zeros((n_wells, nz), jnp.float32)
@@ -258,7 +310,7 @@
             preferred_element_type=jnp.float32,
         )
         rate = jnp.sum(
-            perforated * (with_pressure - bhp_ref[t] * without), axis=1, keepdims=True
+            perforated * (with_pressure - bhp[t] * without), axis=1, keepdims=True
         )
         rates = jnp.where(lane == t, rate, rates)
     w_s[...] = rates
@@ -295,9 +347,19 @@
 
     for copy in m_copies:
         copy.wait()
+    slot_index = lax.broadcasted_iota(jnp.int32, (1, slots), 1)
+    scale = jnp.concatenate(
+        [
+            jnp.where(
+                slot_index < fault_count_ref[:, p : p + 1], fault_trans_ref[0, p : p + 1, :], 0.0
+            )
+            for p in range(peers)
+        ],
+        axis=1,
+    )
+    fault_up = as_row(fault_up_ref)
     for t in range(2):
-        own_up = jnp.bitwise_and(jnp.right_shift(fault_up_ref[...], t), 1) == 1
-        scale = fault_trans_ref[...] * fault_live_ref[...]
+        own_up = jnp.bitwise_and(jnp.right_shift(fault_up, t), 1) == 1
         for k in range(3):
             q = 3 * t + k
             other = jnp.concatenate([m_r[p, q : q + 1, :] for p in range(peers)], axis=1)
@@ -305,18 +367,20 @@
 
     for copy in w_copies:
         copy.wait()
+    for load in loads[4:]:
+        load.wait()
     rates = w_s[...]
     for offset in range(1, n_gz):
         rates = rates + w_r[offset]
     explicit_sum = jnp.zeros(shape, jnp.float32)
     for t in range(2):
-        misfit = (rates[:, t : t + 1] - obs_ref[t]) / sigma_sq
+        misfit = (rates[:, t : t + 1] - as_column(obs_ref[t, 0])) / sigma_sq
         weight = misfit * perforated
         spread = jnp.dot(
             well_hot_t, weight, precision=HIGHEST, preferred_element_type=jnp.float32
         ).reshape(shape)
         spread_bhp = jnp.dot(
-            well_hot_t, weight * bhp_ref[t], precision=HIGHEST, preferred_element_type=jnp.float32
+            well_hot_t, weight * bhp[t], precision=HIGHEST, preferred_element_type=jnp.float32
         ).reshape(shape)
         drawn = pressure[t] * spread - spread_bhp
         water_slope, oil_slope = mobility_slopes(
@@ -411,7 +475,7 @@
             copy.wait()
         arrived = jnp.concatenate([c_r[slot, p] for p in range(peers)], axis=1)
         picked = jnp.where(
-            lax.broadcasted_iota(jnp.int32, (rows, wide), 0) == fault_row_ref[...], arrived, 0.0
+            lax.broadcasted_iota(jnp.int32, (rows, wide), 0) == fault_row, arrived, 0.0
         )
         both = jnp.concatenate(split_bf16(picked), axis=0)
         added = lax.dot_general(
@@ -470,14 +534,86 @@
         lax.broadcasted_iota(jnp.int32, (nz, nz), 0) // BOX
         == lax.broadcasted_iota(jnp.int32, (nz, nz), 1)
     ).astype(jnp.float32)
-    for q, field in enumerate((explicit[...], -porosity_sum)):
+    n_boxes = nx * ny // BOX**2
+    xy_boxes = (
+        lax.broadcasted_iota(jnp.int32, (n_boxes, nx // BOX * ny), 1) // BOX
+        == lax.broadcasted_iota(jnp.int32, (n_boxes, nx // BOX * ny), 0)
+    ).astype(jnp.float32)
+    boxes = []
+    for field in (explicit[...], -porosity_sum):
         in_x = jnp.sum(field.reshape(nx // BOX, BOX, ny, nz), axis=1)
-        box_ref[q] = jnp.dot(
+        in_z = jnp.dot(
             in_x.reshape(nx // BOX * ny, nz),
             z_boxes,
             precision=HIGHEST,
             preferred_element_type=jnp.float32,
         )
+        boxes.append(
+            jnp.dot(xy_boxes, in_z, precision=HIGHEST, preferred_element_type=jnp.float32)
+        )
+    boxes = jnp.concatenate(boxes, axis=0)[:, : nz // BOX]
+    box_row = lax.rem(lax.broadcasted_iota(jnp.int32, boxes.shape, 0), n_boxes)
+    share = peers * PARAM_REGIONS
+    labels = lax.broadcasted_iota(jnp.int32, (n_gx * share, nz // BOX), 0)
+    found = jnp.zeros((4 * n_boxes, n_gx * share), jnp.float32)
+    for b in range(n_boxes):
+        y_box = b % (ny // BOX)
+        region = map_ref[b // (ny // BOX), y_box : y_box + 1, :]
+        found = found + lax.dot_general(
+            jnp.concatenate(split_bf16(jnp.where(box_row == b, boxes, 0.0)), axis=0),
+            (labels == region).astype(jnp.float32).astype(jnp.bfloat16),
+            (((1,), (1,)), ((), ())),
+            preferred_element_type=jnp.float32,
+        )
+    found = found[: 2 * n_boxes] + found[2 * n_boxes :]
+    for q in range(2):
+        of_q = jnp.sum(found[q * n_boxes : (q + 1) * n_boxes], axis=0, keepdims=True)
+        for g in range(n_gx):
+            g_s[g, q : q + 1, :] = of_q[:, g * share : (g + 1) * share]
+    g_copies = []
+    for offset in range(1, n_gx):
+        copy = remote(
+            g_s.at[lax.rem(here[0] + offset, n_gx)],
+            g_r.at[offset],
+            g_ss.at[offset],
+            g_rs.at[offset],
+            toward(0, offset),
+        )
+        copy.start()
+        g_copies.append(copy)
+    for copy in g_copies:
+        copy.wait()
+    part = g_s[here[0]]
+    for offset in range(1, n_gx):
+        part = part + g_r[offset]
+    lanes = r_s.shape[2]
+    together = lanes // PARAM_REGIONS
+    for p in range(peers):
+        first = p // together * lanes
+        r_s[p] = part[:, first : first + lanes]
+    r_copies = []
+    for offset in range(1, peers):
+        copy = remote(
+            r_s.at[lax.rem(me + offset, peers)],
+            r_r.at[offset],
+            r_ss.at[offset],
+            r_rs.at[offset],
+            peer(offset),
+        )
+        copy.start()
+        r_copies.append(copy)
+    for copy in r_copies:
+        copy.wait()
+    part = r_s[me]
+    for offset in range(1, peers):
+        part = part + r_r[offset]
+    mine = jnp.full((2, PARAM_REGIONS), lax.rem(me, together), jnp.int32)
+    result = jnp.zeros((2, PARAM_REGIONS), jnp.float32)
+    for n in range(together):
+        result = jnp.where(
+            mine == n, part[:, n * PARAM_REGIONS : (n + 1) * PARAM_REGIONS], result
+        )
+    region_ref[...] = result
 
 
 def local(
@@ -505,17 +641,20 @@
     peers, slots = fault_cell.shape[1:]
     wide = peers * slots
     n_wells = well_x.shape[2]
-    well_row = well_x[0, 0] * ny + well_y[0, 0]
-    cells = fault_cell[0]
-    live = (
-        jnp.arange(slots, dtype=jnp.int32)[None, :] < fault_count[0][:, None]
-    ).astype(jnp.float32)
+    hbm = pl.BlockSpec(memory_space=pltpu.HBM)
     vmem = pl.BlockSpec(memory_space=pltpu.VMEM)
     f32 = jnp.float32
     dma = pltpu.SemaphoreType.DMA
     faces = [(2, ny, nz), (2, nx, 1, nz), (2, ny, nz)]
     bundles = [(2, 10, ny, nz), (2, 10, nx, 1, nz), (2, 10, ny, nz)]
+    lanes = 128
+    share = peers * PARAM_REGIONS
+    large = (
+        pressure, saturation, permeability, porosity, upwind_flags, diag_inverse, seismic_obs
+    )
     scratch = [
+        *[pltpu.VMEM(array.shape, array.dtype) for array in large],
+        dma((len(large),)),
         pltpu.VMEM((2, 3, 3, nx, ny, nz), f32),
         pltpu.VMEM((2, 3, 3, nx, ny, nz), f32),
         pltpu.VMEM((2, 3, nx, ny, nz), f32),
@@ -543,50 +682,41 @@
         pltpu.VMEM((2, peers, 1, slots), f32),
         dma((peers,)),
         dma((2, peers)),
+        pltpu.VMEM((counts[0], 2, share), f32),
+        pltpu.VMEM((counts[0], 2, share), f32),
+        dma((counts[0],)),
+        dma((counts[0],)),
+        pltpu.VMEM((peers, 2, lanes), f32),
+        pltpu.VMEM((peers, 2, lanes), f32),
+        dma((peers,)),
+        dma((peers,)),
     ]
-    adjoint, boxes = pl.pallas_call(
+    return pl.pallas_call(
         functools.partial(kernel, counts),
         out_shape=(
             jax.ShapeDtypeStruct((2, 3, nx, ny, nz), f32),
-            jax.ShapeDtypeStruct((2, nx // BOX * ny, nz), f32),
+            jax.ShapeDtypeStruct((2, PARAM_REGIONS), f32),
         ),
-        in_specs=[vmem] * 18,
+        in_specs=[hbm] * 7 + [vmem] * 11,
         out_specs=(vmem, vmem),
         scratch_shapes=scratch,
         compiler_params=pltpu.CompilerParams(
-            collective_id=0, has_side_effects=True, vmem_limit_bytes=48 * 2**20
+            collective_id=0, has_side_effects=True, vmem_limit_bytes=63 * 2**20
         ),
     )(
-        pressure,
-        saturation,
-        permeability,
-        porosity,
-        upwind_flags,
-        diag_inverse,
-        seismic_obs,
-        well_row[:, None],
-        well_row[None, :],
-        well_top[0, 0][:, None],
-        well_len[0, 0][:, None],
-        well_bhp[:, 0, 0][:, :, None],
-        well_obs[:, 0, 0][:, :, None],
-        (cells // nz).reshape(1, wide),
-        (cells % nz).reshape(1, wide),
-        fault_trans[0].reshape(1, wide),
-        fault_up[0].reshape(1, wide),
-        live.reshape(1, wide),
-    )
-    box_totals = boxes[:, :, : nz // BOX].reshape(2, nx // BOX, ny // BOX, BOX, nz // BOX)
-    box_totals = jnp.sum(box_totals, axis=3).reshape(2, -1)
-    region_labels = PARAM_REGIONS * counts[0] * counts[1] * counts[2]
-    chosen = (
-        region_map.reshape(-1)[:, None] == jnp.arange(region_labels, dtype=jnp.int32)[None, :]
-    ).astype(f32)
-    region_partial = jnp.dot(box_totals, chosen, precision=HIGHEST)
-    region_grad = lax.psum_scatter(
-        region_partial, ("gx", "gy", "gz"), scatter_dimension=1, tiled=True
-    )
-    return (adjoint, region_grad)
+        *large,
+        well_x,
+        well_y,
+        well_top,
+        well_len,
+        well_bhp,
+        well_obs,
+        fault_cell,
+        fault_count,
+        fault_trans,
+        fault_up,
+        region_map,
+    )
 
 
 def solution(mesh):

time: 244 us -> 90.7 us (0.37)
  waiting for transfers between devices: 133 us -> 0 us
  between operations: 14.1 us -> 0.65 us
  local copies, waits for them, and re-layouts: 14 us -> 2.96 us
  Pallas kernels: 76.4 us -> 86.9 us
  other arithmetic: 2.9 us -> 0 us
    unnamed x2 -> x0, waiting for transfers between devices: 133 us -> none
    pallas_call x1, Pallas kernels: 76.4 us -> 86.9 us  [local(): pl.pallas_call(functools.partial(kernel, counts), out_shape=(jax.ShapeDty...]
    unnamed x20 -> x2, local copies, waits for them, and re-layouts: 10 us -> 2.96 us
    another operation x4 -> x0, local copies, waits for them, and re-layouts: 3.04 us -> none  [the longest x1 0.78 us: local(): well_obs[:, 0, 0][:, :, None]]
  transfers between devices with their start and end apart: 1 -> 0, of which waited for: 1 -> 0; matrix products, arithmetic and copies ran while one was open for 0% -> 0% of each run, Pallas kernels for 0% -> 0%
where the time goes in v2:
time: 90.7 us; the launch traced here: 90.5 us
  Pallas kernels  86.9 us (96%)
  local copies, waits for them, and re-layouts  2.96 us (3%)
    pallas_call x1, Pallas kernels, local(): pl.pallas_call(functools.partial(kernel, counts), out_shape=(jax.ShapeDty...  86.9 us
    unnamed x2, local copies, waits for them, and re-layouts  2.96 us

profile of v2, /device:TPU:0, one launch (start us, length us, event | category | flops | bytes accessed | tf_op | source)
XLA Modules:
  0.0 90.5 jit_solution(8668030232521485329)
XLA Ops:
  0.6 86.9 %shard_map.185 = (f32[2,3,16,8,128]{4,3,2,1,0:T(8,128)}, f32[2,32]{1,0:T(2,128)}) custom-call(f32[2,16,8,128]{3,2,1,0:T(8,128)} %pressure_hbm.1, f32[3,2,16,8,128]{4,3,2,1,0:T(8,128)} %saturation_hbm.1, f32[16,8,128]{2,1,0:T(8,128)} %perm_hbm.1, f32[16,8,128]{2,1,0:T(8,128)} %porosity_hbm.1, s32[16,8,128]{2,1,0:T(8,128)} %flags_hbm.1, ...), custom_call_target="tpu_custom_call" | custom-call | tf_op jit(solution)/shard_map/pallas_call | solution.py:694
  87.6 1.8 %copy.22 = f32[2,3,16,8,128]{4,3,2,1,0:T(8,128)} copy(f32[2,3,16,8,128]{4,3,2,1,0:T(8,128)} %get-tuple-element.4) | data formatting | bytes 786432
  89.3 1.2 %copy.23 = f32[2,32]{1,0:T(2,128)} copy(f32[2,32]{1,0:T(2,128)} %get-tuple-element.5) | data formatting | bytes 512

commit v3 on v2

--- a/solution.py
+++ b/solution.py
@@ -445,11 +445,7 @@
     def sweep(t, n_face, n_fault):
         face_slot = lax.rem(n_face, 2)
         slot = lax.rem(n_fault, 2)
-        lam, up, down = products(t)
-        faces = face_copies(face_slot)
-        for copy in faces:
-            copy.start()
-        values = gather(lam)
+        values = gather([lam_ref[t, k] for k in range(3)])
         sent = sum(
             fault_coef[3 * t + k : 3 * t + k + 1, :] * values[k] for k in range(3)
         )
@@ -467,6 +463,10 @@
             )
             copy.start()
             copies.append(copy)
+        lam, up, down = products(t)
+        faces = face_copies(face_slot)
+        for copy in faces:
+            copy.start()
         for copy in faces:
             copy.wait()
         upper, lower = terms(up, down, face_slot)
@@ -489,11 +489,8 @@
 
     log_perm = explicit_sum
     for turn, t in enumerate((1, 0)):
-        if t == 0:
-            porosity = porosity_ref[...]
-            src[0, 1] += porosity * (lam_ref[1, 0] - lam_ref[1, 2])
-            src[0, 2] += porosity * (lam_ref[1, 1] - lam_ref[1, 2])
-        relax(t, None)
+        if t == 1:
+            relax(1, None)
 
         def body(step, carry, t=t, turn=turn):
             sweep(t, turn * ITERS + step, turn * (ITERS - 1) + step)
@@ -505,6 +502,19 @@
         faces = face_copies(slot)
         for copy in faces:
             copy.start()
+        if t == 0:
+            porosity_sum = jnp.zeros(shape, jnp.float32)
+            for at in range(2):
+                water = saturation_ref[at + 1, 0] - saturation_ref[at, 0]
+                oil = saturation_ref[at + 1, 1] - saturation_ref[at, 1]
+                porosity_sum = porosity_sum + (
+                    lam_ref[at, 0] * water + lam_ref[at, 1] * oil - lam_ref[at, 2] * (water + oil)
+                )
+        else:
+            porosity = porosity_ref[...]
+            src[0, 1] += porosity * (lam[0] - lam[2])
+            src[0, 2] += porosity * (lam[1] - lam[2])
+            relax(0, None)
         for copy in faces:
             copy.wait()
         upper, lower = terms(up, down, slot)
@@ -523,13 +533,6 @@
             )
         explicit[...] -= flux
 
-    porosity_sum = jnp.zeros(shape, jnp.float32)
-    for t in range(2):
-        water = saturation_ref[t + 1, 0] - saturation_ref[t, 0]
-        oil = saturation_ref[t + 1, 1] - saturation_ref[t, 1]
-        porosity_sum = porosity_sum + (
-            lam_ref[t, 0] * water + lam_ref[t, 1] * oil - lam_ref[t, 2] * (water + oil)
-        )
     z_boxes = (
         lax.broadcasted_iota(jnp.int32, (nz, nz), 0) // BOX
         == lax.broadcasted_iota(jnp.int32, (nz, nz), 1)

time: 90.7 us -> 90.4 us (level)
  no operation moved by 1% of the time
where the time goes in v3:
time: 90.4 us; the launch traced here: 90.2 us
  Pallas kernels  86.6 us (96%)
  local copies, waits for them, and re-layouts  2.96 us (3%)
    pallas_call x1, Pallas kernels, local(): pl.pallas_call(functools.partial(kernel, counts), out_shape=(jax.ShapeDty...  86.6 us
    unnamed x2, local copies, waits for them, and re-layouts  2.96 us

profile of v3, /device:TPU:0, one launch (start us, length us, event | category | flops | bytes accessed | tf_op | source)
XLA Modules:
  0.0 90.2 jit_solution(17245169864270285365)
XLA Ops:
  0.6 86.6 %shard_map.185 = (f32[2,3,16,8,128]{4,3,2,1,0:T(8,128)}, f32[2,32]{1,0:T(2,128)}) custom-call(f32[2,16,8,128]{3,2,1,0:T(8,128)} %pressure_hbm.1, f32[3,2,16,8,128]{4,3,2,1,0:T(8,128)} %saturation_hbm.1, f32[16,8,128]{2,1,0:T(8,128)} %perm_hbm.1, f32[16,8,128]{2,1,0:T(8,128)} %porosity_hbm.1, s32[16,8,128]{2,1,0:T(8,128)} %flags_hbm.1, ...), custom_call_target="tpu_custom_call" | custom-call | tf_op jit(solution)/shard_map/pallas_call | solution.py:697
  87.3 1.8 %copy.22 = f32[2,3,16,8,128]{4,3,2,1,0:T(8,128)} copy(f32[2,3,16,8,128]{4,3,2,1,0:T(8,128)} %get-tuple-element.4) | data formatting | bytes 786432
  89.0 1.2 %copy.23 = f32[2,32]{1,0:T(2,128)} copy(f32[2,32]{1,0:T(2,128)} %get-tuple-element.5) | data formatting | bytes 512

commit v4 on v3

--- a/solution.py
+++ b/solution.py
@@ -474,10 +474,10 @@
         for copy in copies:
             copy.wait()
         arrived = jnp.concatenate([c_r[slot, p] for p in range(peers)], axis=1)
-        picked = jnp.where(
-            lax.broadcasted_iota(jnp.int32, (rows, wide), 0) == fault_row, arrived, 0.0
-        )
-        both = jnp.concatenate(split_bf16(picked), axis=0)
+        hot = row_hot[:rows]
+        both = jnp.concatenate(
+            [hot * jnp.broadcast_to(part, hot.shape) for part in split_bf16(arrived)], axis=0
+        )
         added = lax.dot_general(
             both,
             z_hot[...],

time: 90.4 us -> 90.3 us (level)
  no operation moved by 1% of the time
where the time goes in v4:
time: 90.3 us; the launch traced here: 90 us
  Pallas kernels  86.4 us (96%)
  local copies, waits for them, and re-layouts  2.96 us (3%)
    pallas_call x1, Pallas kernels, local(): pl.pallas_call(functools.partial(kernel, counts), out_shape=(jax.ShapeDty...  86.4 us
    unnamed x2, local copies, waits for them, and re-layouts  2.96 us

profile of v4, /device:TPU:0, one launch (start us, length us, event | category | flops | bytes accessed | tf_op | source)
XLA Modules:
  0.0 90.0 jit_solution(3050669998386155057)
XLA Ops:
  0.6 86.4 %shard_map.185 = (f32[2,3,16,8,128]{4,3,2,1,0:T(8,128)}, f32[2,32]{1,0:T(2,128)}) custom-call(f32[2,16,8,128]{3,2,1,0:T(8,128)} %pressure_hbm.1, f32[3,2,16,8,128]{4,3,2,1,0:T(8,128)} %saturation_hbm.1, f32[16,8,128]{2,1,0:T(8,128)} %perm_hbm.1, f32[16,8,128]{2,1,0:T(8,128)} %porosity_hbm.1, s32[16,8,128]{2,1,0:T(8,128)} %flags_hbm.1, ...), custom_call_target="tpu_custom_call" | custom-call | tf_op jit(solution)/shard_map/pallas_call | solution.py:697
  87.1 1.8 %copy.22 = f32[2,3,16,8,128]{4,3,2,1,0:T(8,128)} copy(f32[2,3,16,8,128]{4,3,2,1,0:T(8,128)} %get-tuple-element.4) | data formatting | bytes 786432
  88.8 1.2 %copy.23 = f32[2,32]{1,0:T(2,128)} copy(f32[2,32]{1,0:T(2,128)} %get-tuple-element.5) | data formatting | bytes 512
